TPU v7x, 256 devices: a whole 4x4x8 slice. The times are simulated.
256 devices in a mesh: ctx: 16 (over z, core), row: 4 (over x), col: 4 (over y).
Axes of the slice: x: 4, y: 4, z: 8, core: 2. Of those that a mesh axis runs over, the one named last changes fastest.
Arguments:
- projected: bfloat16 [16384, 8704], P(('ctx', 'row'), 'col'), may hold values from -6 to 6
- conv_taps: float32 [3, 8704], P(None, 'col'), may hold values from -3 to 3
- out_weight: bfloat16 [8192, 8192], P('col', 'row'), may hold values from -0.0625 to 0.0625
Outputs:
- output: bfloat16 [16384, 8192], P(('ctx', 'col'), 'row')
All inputs are finite; a program needn't handle non-finite values.
Results may differ from a plain program's by a relative error of at most 0.02.
Values may be sent and summed in bfloat16 or wider, within the bound.
A program may use at most 192 MiB of HBM per device.

v0:
```python
import jax
import jax.numpy as jnp
import numpy as np
from jax import lax
from jax.sharding import PartitionSpec as P

FEAT = 16
DV = 512
PHI = 153


def from_behind(value, axis, by):
    length = lax.axis_size(axis)
    pairs = [(i, i + by) for i in range(length) if 0 <= i + by < length]
    return lax.ppermute(value, axis, pairs)


def entering(value, axis, join, neutral):
    place = lax.axis_index(axis)
    gathered = jax.tree.map(
        lambda a, kind: lax.all_gather(a.astype(kind), axis),
        value,
        jax.tree.map(lambda a: jnp.bfloat16 if a.dtype == jnp.float32 else a.dtype, value),
    )
    state = jax.tree.map(lambda a, e: jnp.zeros_like(a) + jnp.asarray(e, a.dtype), value, neutral)

    def one(step, state):
        return join(
            state,
            jax.tree.map(
                lambda a, own: lax.dynamic_index_in_dim(a, step, 0, False).astype(own.dtype),
                gathered,
                value,
            ),
        )

    return lax.fori_loop(0, place, one, state)


def features(values):
    width = values.shape[-1]
    first, second = np.triu_indices(width)
    coef = np.where(first == second, (2.0 * width) ** (-0.5), width ** (-0.5)).astype(np.float32)
    ones = jnp.ones(values.shape[:-1] + (1,), values.dtype)
    quad = values[..., first] * values[..., second] * coef
    return jnp.concatenate([ones, values * width ** (-0.25), quad], axis=-1)


def combine(earlier, later):
    return (earlier[0] + later[0], earlier[1] + later[1])


def shards(projected, conv_taps, out_weight):
    width = 2 * FEAT + DV
    heads = projected.shape[1] // width
    rows = projected.shape[0]
    tail = from_behind(projected[-2:], ("ctx", "row"), 1)
    extended = jnp.concatenate([tail, projected], axis=0).astype(jnp.float32)
    convolved = (
        conv_taps[0] * extended[2:] + conv_taps[1] * extended[1:-1] + conv_taps[2] * extended[:-2]
    )
    gated = (extended[2:] * convolved).astype(jnp.bfloat16).reshape(rows, heads, width)
    query = gated[..., :FEAT]
    key = gated[..., FEAT : 2 * FEAT]
    value = gated[..., 2 * FEAT :]
    causal = jnp.arange(rows)[:, None] >= jnp.arange(rows)[None, :]
    scores = jnp.einsum("thi,shi->hts", query, key, preferred_element_type=jnp.float32) * FEAT ** (
        -0.5
    )
    kernel = jnp.where(causal[None], 1.0 + scores + 0.5 * scores * scores, 0.0).astype(jnp.bfloat16)
    num_in = jnp.einsum("hts,shd->thd", kernel, value, preferred_element_type=jnp.float32)
    den_in = jnp.sum(kernel.astype(jnp.float32), axis=-1).T
    value_wide = value.astype(jnp.float32)
    phi_query = features(query.astype(jnp.float32))
    phi_key = features(key.astype(jnp.float32))
    local_num = jnp.einsum(
        "thf,thd->fhd", phi_key, value_wide, precision=lax.Precision.HIGHEST
    ).reshape(PHI, heads * DV)
    local_den = jnp.sum(phi_key, axis=0)
    zero_num = jnp.zeros((PHI, heads * DV), jnp.float32)
    zero_den = jnp.zeros((heads, PHI), jnp.float32)
    group_num, group_den = (
        lax.psum(local_num.astype(jnp.bfloat16), "row").astype(jnp.float32),
        lax.psum(local_den.astype(jnp.bfloat16), "row").astype(jnp.float32),
    )
    inner_num, inner_den = entering((local_num, local_den), "row", combine, (zero_num, zero_den))
    position = lax.axis_index("ctx")
    pieces = (
        lax.all_gather(group_num[None].astype(jnp.bfloat16), "ctx", axis=0, tiled=True).astype(
            jnp.float32
        ),
        lax.all_gather(group_den[None].astype(jnp.bfloat16), "ctx", axis=0, tiled=True).astype(
            jnp.float32
        ),
    )
    keep = jnp.arange(pieces[0].shape[0], dtype=jnp.int32) < position
    summed_num = jnp.sum(jnp.where(keep[:, None, None], pieces[0], 0.0), axis=0)
    summed_den = jnp.sum(jnp.where(keep[:, None, None], pieces[1], 0.0), axis=0)
    outer_num = zero_num + summed_num
    outer_den = zero_den + summed_den
    prior_num = outer_num + inner_num
    prior_den = outer_den + inner_den
    num_out = jnp.einsum(
        "thf,fhd->thd",
        phi_query,
        prior_num.reshape(PHI, heads, DV),
        precision=lax.Precision.HIGHEST,
    )
    den_out = jnp.einsum("thf,hf->th", phi_query, prior_den, precision=lax.Precision.HIGHEST)
    attended = (
        ((num_out + num_in) / (den_out + den_in)[..., None])
        .astype(jnp.bfloat16)
        .reshape(rows, heads * DV)
    )
    partial_out = jnp.dot(
        lax.all_gather(attended, "row", axis=0, tiled=True),
        out_weight,
        preferred_element_type=jnp.float32,
    ).astype(jnp.bfloat16)
    summed = lax.psum_scatter(
        partial_out.astype(jnp.float32).astype(jnp.bfloat16), "col", scatter_dimension=0, tiled=True
    )
    return summed


def solution(mesh):
    in_specs = (P(("ctx", "row"), "col"), P(None, "col"), P("col", "row"))
    out_specs = P(("ctx", "col"), "row")
    return jax.shard_map(shards, mesh=mesh, in_specs=in_specs, out_specs=out_specs, check_vma=False)
```

profile of v0, /device:TPU:1, one launch (start us, length us, event | category | flops | bytes accessed | tf_op | source)
XLA Modules:
  0.0 324.0 jit_solution(8538381725146888905)
XLA Ops:
  6.5 0.8 slice.31
  7.3 3.9 %collective-permute-start = (bf16[2,2176]{1,0:T(2,128)(2,1)S(1)}, bf16[2,2176]{1,0:T(2,128)(2,1)S(1)}, u32[]{:S(2)}, u32[]{:S(2)}) collective-permute-start(bf16[2,2176]{1,0:T(2,128)(2,1)S(1)} %slice.31), channel_id=1, source_target_pairs={{0,4},{4,8},{8,12},{12,16},{16,20},{20,24},{24,28},{28,32},{32,36}... | collective-permute-start | bytes 26120 | tf_op jit(solution)/shard_map/ppermute | solution.py:15
  11.3 0.9 slice_reduce_fusion.2
  12.2 0.7 pad_clamp_fusion.1
  12.9 0.7 pad_clamp_fusion
  13.6 0.8 collective-permute-done
  14.4 1.5 maximum_convert_fusion
  15.9 0.8 fusion.2
  16.7 0.7 copy.31
  17.5 0.9 gather_fusion
  18.4 0.9 gather_fusion.1
  19.3 0.0 copy-start.3
  19.4 0.9 gather_fusion.2
  20.3 0.9 gather_fusion.3
  21.3 0.4 fusion.11
  21.6 0.9 copy-done.1
  22.5 1.2 fusion.7
  23.7 0.5 copy.37
  24.2 1.2 convert_element_type.96
  25.4 0.0 all-gather.8.cloned.1.call-update
  25.5 40.4 %all-gather.8.cloned.1.call-done = bf16[4,153,2048]{2,1,0:T(8,128)(2,1)} async-done(((bf16[1,153,2048]{2,1,0:T(8,128)(2,1)}), bf16[4,153,2048]{2,1,0:T(8,128)(2,1)}) %all-gather.8.cloned.1.call-update) | async-done | bytes 2506768 | tf_op jit(solution)/shard_map/all_gather | solution.py:21
  65.9 0.7 all-reduce.2.cloned.1.call-update
  66.6 0.0 all-gather.6.cloned.1.call-start
  66.6 49.5 %all-reduce.2.cloned.1.call-done = bf16[1,153,2048]{2,1,0:T(8,128)(2,1)} async-done(((bf16[1,153,2048]{2,1,0:T(8,128)(2,1)}), bf16[1,153,2048]{2,1,0:T(8,128)(2,1)}) %all-reduce.2.cloned.1.call-update) | async-done | bytes 626704 | tf_op jit(solution)/shard_map/psum | solution.py:83
  116.1 0.0 all-gather.6.cloned.1.call-update
  116.1 0.0 all-gather.10.cloned.1.call-start
  116.2 0.3 fusion.15
  116.6 8.2 %psum.15 = bf16[1,4,153]{2,1,0:T(4,128)(2,1)S(1)} all-reduce(bf16[1,4,153]{2,1,0:T(4,128)(2,1)S(1)} %bitcast.43), channel_id=1, replica_groups=mesh['ctx'=16,'row'=4,'col'=4] {'row'}, use_global_device_ids=true, to_apply=%region_5.6 | all-reduce | flops 612 | bytes 2448 | tf_op jit(solution)/shard_map/psum | solution.py:84
  124.8 8.1 %all-gather.1 = bf16[4,4,153]{2,1,0:T(4,128)(2,1)S(1)} all-gather(bf16[1,4,153]{2,1,0:T(4,128)(2,1)S(1)} %bitcast.44), channel_id=2, replica_groups=mesh['ctx'=16,'row'=4,'col'=4] {'row'}, dimensions={0}, use_global_device_ids=true | all-gather | bytes 6120 | tf_op jit(solution)/shard_map/all_gather | solution.py:21
  132.9 23.5 %all_gather.20 = bf16[16,4,153]{2,1,0:T(4,128)(2,1)S(1)} all-gather(bf16[1,4,153]{2,1,0:T(4,128)(2,1)S(1)} %psum.15), channel_id=1, replica_groups=mesh['ctx'=16,'row'=4,'col'=4] {'ctx'}, dimensions={0}, use_global_device_ids=true | all-gather | bytes 20808 | tf_op jit(solution)/shard_map/all_gather | solution.py:92
  156.4 0.1 select_reduce_fusion.1
  156.5 2.1 convert_reduce_fusion
  158.5 0.1 broadcast_in_dim.68
  158.7 0.2 while.12
  158.9 0.5 fusion.14
  159.4 27.6 %all-gather.6.cloned.1.call-done = bf16[16,153,2048]{2,1,0:T(8,128)(2,1)} async-done(((bf16[1,153,2048]{2,1,0:T(8,128)(2,1)}), bf16[16,153,2048]{2,1,0:T(8,128)(2,1)}) %all-gather.6.cloned.1.call-update) | async-done | bytes 10027024 | tf_op jit(solution)/shard_map/all_gather | solution.py:89
  187.0 6.8 %select_reduce_fusion = f32[153,2048]{1,0:T(8,128)S(1)} fusion(bf16[16,153,2048]{2,1,0:T(8,128)(2,1)} %all-gather.6.cloned.1.call-done, pred[16]{0:T(512)(128)(4,1)S(1)} %iota_compare_fusion.1), kind=kLoop, calls=%fused_computation.6 | loop fusion | flops 14727168 | bytes 11280400 | tf_op jit(solution)/shard_map/reduce_sum | solution.py:97
  193.8 0.2 add.70
  194.0 0.8 reshape.56
  194.9 0.0 copy-start.4
  194.9 3.7 %fusion.5 = f32[4,512,256]{2,1,0:T(8,128)S(1)} fusion(f32[153,4,512]{2,1,0:T(4,128)S(1)} %reshape.56, f32[256,4,136]{0,2,1:T(8,128)S(1)} %get-tuple-element.60, f32[256,4,16]{0,2,1:T(8,128)S(1)} %get-tuple-element.56, f32[153]{0:T(256)S(1)} %pad.3.clone), kind=kOutput, calls=%fused_computation.17 | convolution fusion | flops 962906112 | bytes 3973732 | tf_op jit(solution)/shard_map/thf,fhd->thd/dot_general | solution.py:103
  198.6 1.4 fusion.4
  200.0 0.0 all-gather.10.cloned.1.call-update
  200.1 0.3 reduce-scatter.2.cloned.1.call-start
  200.3 51.7 %all-gather.10.cloned.1.call-done = bf16[1024,2048]{0,1:T(8,128)(2,1)} async-done(((bf16[256,2048]{0,1:T(8,128)(2,1)}), bf16[1024,2048]{0,1:T(8,128)(2,1)}) %all-gather.10.cloned.1.call-update) | async-done | bytes 4194320 | tf_op jit(solution)/shard_map/all_gather | solution.py:116
  252.0 14.0 %convolution_convert_fusion = bf16[1024,2048]{1,0:T(8,128)(2,1)} fusion(bf16[1024,2048]{0,1:T(8,128)(2,1)} %all-gather.10.cloned.1.call-done, bf16[2048,2048]{1,0:T(8,128)(2,1)} %param.17), kind=kOutput, calls=%fused_computation.7 | convolution fusion | flops 8592031744 | bytes 16777216 | tf_op jit(solution)/shard_map/dot_general | solution.py:115
  266.0 0.0 reduce-scatter.2.cloned.1.call-update
  266.0 51.4 %reduce-scatter.2.cloned.1.call-done = bf16[256,2048]{1,0:T(8,128)(2,1)} async-done(((bf16[1024,2048]{1,0:T(8,128)(2,1)}), bf16[256,2048]{1,0:T(8,128)(2,1)}) %reduce-scatter.2.cloned.1.call-update) | async-done | bytes 1048592 | tf_op jit(solution)/shard_map/reduce_scatter | solution.py:120
  (19 shorter events, 0.2 us)
Async XLA Ops:
  6.5 59.3 %all-gather.8.cloned.1.call-start = ((), (), s32[]{:S(2)}) async-start(), calls=%async_computation.3 | async-start | bytes 3276800 | tf_op jit(solution)/shard_map/all_gather | solution.py:21
  7.3 7.1 %collective-permute-start = (bf16[2,2176]{1,0:T(2,128)(2,1)S(1)}, bf16[2,2176]{1,0:T(2,128)(2,1)S(1)}, u32[]{:S(2)}, u32[]{:S(2)}) collective-permute-start(bf16[2,2176]{1,0:T(2,128)(2,1)S(1)} %slice.31), channel_id=1, source_target_pairs={{0,4},{4,8},{8,12},{12,16},{16,20},{20,24},{24,28},{28,32},{32,36}... | collective-permute-start | bytes 26120 | tf_op jit(solution)/shard_map/ppermute | solution.py:15
  17.4 3.8 %copy-start = (bf16[256,2176]{0,1:T(8,128)(2,1)}, bf16[256,2176]{0,1:T(8,128)(2,1)S(1)}, u32[]{:S(2)}) copy-start(bf16[256,2176]{0,1:T(8,128)(2,1)S(1)} %copy.31) | copy-start | bytes 3342340
  19.3 1.9 copy-start.3
  21.2 1.2 copy-start.1
  65.9 50.2 %all-reduce.2.cloned.1.call-start = ((), (), s32[]{:S(2)}) async-start(), calls=%async_computation.1 | async-start | bytes 1310720 | tf_op jit(solution)/shard_map/psum | solution.py:83
  66.6 120.4 %all-gather.6.cloned.1.call-start = ((), (), s32[]{:S(2)}) async-start(), calls=%async_computation.2 | async-start | bytes 11141120 | tf_op jit(solution)/shard_map/all_gather | solution.py:89
  116.1 135.8 %all-gather.10.cloned.1.call-start = ((), (), s32[]{:S(2)}) async-start(), calls=%async_computation.4 | async-start | bytes 5242880 | tf_op jit(solution)/shard_map/all_gather | solution.py:116
  194.9 3.7 %copy-start.2 = (bf16[256,2176]{0,1:T(8,128)(2,1)S(1)}, bf16[256,2176]{0,1:T(8,128)(2,1)}, u32[]{:S(2)}) copy-start(bf16[256,2176]{0,1:T(8,128)(2,1)} %copy-done) | copy-start | bytes 3342340
  194.9 3.7 %copy-start.4 = (bf16[4,256,256]{1,2,0:T(8,128)(2,1)S(1)}, bf16[4,256,256]{1,2,0:T(8,128)(2,1)}, u32[]{:S(2)}) copy-start(bf16[4,256,256]{1,2,0:T(8,128)(2,1)} %get-tuple-element.63) | copy-start | bytes 1572868
  200.1 117.4 %reduce-scatter.2.cloned.1.call-start = ((), (), s32[]{:S(2)}) async-start(), calls=%async_computation.5 | async-start | bytes 5242880 | tf_op jit(solution)/shard_map/reduce_scatter | solution.py:120
Sparse Core Ops, SparseCore 0:
  25.6 40.2 all-gather.7
  69.0 47.0 all-reduce.1
  117.9 68.9 all-gather.5
  200.2 51.7 all-gather.9
  266.2 51.2 reduce-scatter.1
where the time goes:
time: 325 us; the launch traced here: 324 us
  waiting for transfers between devices  222 us (68%)
  blocking collectives  39.8 us (12%)
  matrix products  23 us (7%)
  between operations  13.4 us (4%)
  other arithmetic  11.5 us (4%)
  local copies, waits for them, and re-layouts  9.74 us (3%)
  starting transfers between devices  4.29 us (1%)
    all_gather x1, waiting for transfers between devices, shards(): lax.all_gather(attended, 'row', axis=0, tiled=True)  51.7 us
    reduce_scatter x1, waiting for transfers between devices, shards(): lax.psum_scatter(partial_out.astype(jnp.float32).astype(jnp.bfloat16), 'c...  51.4 us
    psum x1, waiting for transfers between devices, shards(): lax.psum(local_num.astype(jnp.bfloat16), 'row').astype(jnp.float32)  49.5 us
    all_gather x1, waiting for transfers between devices, entering(): lax.all_gather(a.astype(kind), axis)  40.4 us
    all_gather x1, waiting for transfers between devices, shards(): lax.all_gather(group_num[None].astype(jnp.bfloat16), 'ctx', axis=0, tiled...  27.6 us
    all_gather x1, blocking collectives, shards(): lax.all_gather(group_den[None].astype(jnp.bfloat16), 'ctx', axis=0, tiled...  23.5 us
    dot_general x1, matrix products, shards(): jnp.dot(lax.all_gather(attended, 'row', axis=0, tiled=True), out_weight,...  14 us
    psum x1, blocking collectives, shards(): lax.psum(local_den.astype(jnp.bfloat16), 'row').astype(jnp.float32)  8.23 us
  transfers between devices with their start and end apart: 6, of which 6 were waited for; matrix products, arithmetic and copies ran while one was open for 2% of the time, Pallas kernels for 0%

commit v1 on v0

--- a/solution.py
+++ b/solution.py
@@ -80,7 +80,7 @@
     zero_num = jnp.zeros((PHI, heads * DV), jnp.float32)
     zero_den = jnp.zeros((heads, PHI), jnp.float32)
     group_num, group_den = (
-        lax.psum(local_num.astype(jnp.bfloat16), "row").astype(jnp.float32),
+        jnp.sum(lax.all_gather(local_num.astype(jnp.bfloat16), "row"), axis=0).astype(jnp.float32),
         lax.psum(local_den.astype(jnp.bfloat16), "row").astype(jnp.float32),
     )
     inner_num, inner_den = entering((local_num, local_den), "row", combine, (zero_num, zero_den))

time: 325 us -> 274 us (0.84)
  waiting for transfers between devices: 222 us -> 170 us
  other arithmetic: 11.5 us -> 15.4 us
    psum x1 -> x0, waiting for transfers between devices: 49.5 us -> none  [shards(): lax.psum(local_num.astype(jnp.bfloat16), 'row').astype(jnp.float32)]
    reduce_sum x0 -> x1, other arithmetic: none -> 3.26 us  [shards(): jnp.sum(lax.all_gather(local_num.astype(jnp.bfloat16), 'row'), axis=0)]
  transfers between devices with their start and end apart: 6 -> 5, of which waited for: 6 -> 5; matrix products, arithmetic and copies ran while one was open for 2% -> 2% of each run, Pallas kernels for 0% -> 0%
where the time goes in v1:
time: 274 us
  waiting for transfers between devices  170 us (62%)
  blocking collectives  37.1 us (14%)
  matrix products  23 us (8%)
  other arithmetic  15.4 us (6%)
  between operations  13.4 us (5%)
  local copies, waits for them, and re-layouts  9.93 us (4%)
  starting transfers between devices  4.3 us (2%)
    all_gather x1, waiting for transfers between devices, shards(): lax.all_gather(attended, 'row', axis=0, tiled=True)  51.7 us
    reduce_scatter x1, waiting for transfers between devices, shards(): lax.psum_scatter(partial_out.astype(jnp.float32).astype(jnp.bfloat16), 'c...  51.4 us
    all_gather x1, waiting for transfers between devices, shards(): lax.all_gather(local_num.astype(jnp.bfloat16), 'row')  40.3 us
    all_gather x1, waiting for transfers between devices, shards(): lax.all_gather(group_num[None].astype(jnp.bfloat16), 'ctx', axis=0, tiled...  26.1 us
    all_gather x1, blocking collectives, shards(): lax.all_gather(group_den[None].astype(jnp.bfloat16), 'ctx', axis=0, tiled...  22.4 us
    dot_general x1, matrix products, shards(): jnp.dot(lax.all_gather(attended, 'row', axis=0, tiled=True), out_weight,...  14 us
    all_gather x1, blocking collectives, entering(): lax.all_gather(a.astype(kind), axis)  8.07 us
    reduce_sum x1, other arithmetic, shards(): summed_num = jnp.sum(jnp.where(keep[:, None, None], pieces[0], 0.0), axis=0)  6.82 us
  transfers between devices with their start and end apart: 5, of which 5 were waited for; matrix products, arithmetic and copies ran while one was open for 2% of the time, Pallas kernels for 0%

profile of v1, /device:TPU:1, one launch (start us, length us, event | category | flops | bytes accessed | tf_op | source)
XLA Modules:
  0.0 273.7 jit_solution(5938771127299813116)
XLA Ops:
  6.5 0.8 slice.31
  7.3 3.9 %collective-permute-start = (bf16[2,2176]{1,0:T(2,128)(2,1)S(1)}, bf16[2,2176]{1,0:T(2,128)(2,1)S(1)}, u32[]{:S(2)}, u32[]{:S(2)}) collective-permute-start(bf16[2,2176]{1,0:T(2,128)(2,1)S(1)} %slice.31), channel_id=1, source_target_pairs={{0,4},{4,8},{8,12},{12,16},{16,20},{20,24},{24,28},{28,32},{32,36}... | collective-permute-start | bytes 26120 | tf_op jit(solution)/shard_map/ppermute | solution.py:15
  11.3 0.7 pad_clamp_fusion.1
  12.0 0.9 slice_reduce_fusion.2
  12.9 0.7 pad_clamp_fusion
  13.6 0.8 collective-permute-done
  14.4 1.5 maximum_convert_fusion
  15.9 0.8 fusion.3
  16.7 0.7 copy.31
  17.4 0.7 broadcast_multiply_fusion
  18.2 0.2 copy-done
  18.4 0.9 gather_fusion.1
  19.3 0.9 gather_fusion
  20.2 0.0 copy-start.5
  20.3 0.9 gather_fusion.2
  21.2 0.9 gather_fusion.3
  22.1 0.4 fusion.12
  22.5 0.9 copy-done.1
  23.4 1.2 fusion.8
  24.6 0.5 copy.37
  25.1 1.2 convert_element_type.93
  26.3 0.0 all-gather.8.cloned.1.call-update
  26.3 0.0 all-gather.12.cloned.1.call-start
  26.4 40.3 %all-gather.8.cloned.1.call-done = bf16[4,153,2048]{2,1,0:T(8,128)(2,1)} async-done(((bf16[1,153,2048]{2,1,0:T(8,128)(2,1)}), bf16[4,153,2048]{2,1,0:T(8,128)(2,1)}) %all-gather.8.cloned.1.call-update) | async-done | bytes 2506768 | tf_op jit(solution)/shard_map/all_gather | solution.py:83
  66.7 3.3 %reduce_sum.50 = bf16[153,2048]{1,0:T(8,128)(2,1)} reduce(bf16[4,153,2048]{2,1,0:T(8,128)(2,1)} %all-gather.8.cloned.1.call-done, bf16[]{:T(256)} %constant.43.clone.1), dimensions={0}, to_apply=%region_0.1 | reduce | flops 940032 | bytes 3133442 | tf_op jit(solution)/shard_map/reduce_sum | solution.py:83
  70.0 0.0 all-gather.12.cloned.1.call-update
  70.0 0.0 all-gather.10.cloned.1.call-start
  70.1 0.3 fusion.16
  70.5 6.6 %psum.7 = bf16[1,4,153]{2,1,0:T(4,128)(2,1)S(1)} all-reduce(bf16[1,4,153]{2,1,0:T(4,128)(2,1)S(1)} %bitcast.45), channel_id=1, replica_groups=mesh['ctx'=16,'row'=4,'col'=4] {'row'}, use_global_device_ids=true, to_apply=%region_5.6 | all-reduce | flops 612 | bytes 2448 | tf_op jit(solution)/shard_map/psum | solution.py:84
  77.0 8.1 %all-gather.3 = bf16[4,4,153]{2,1,0:T(4,128)(2,1)S(1)} all-gather(bf16[1,4,153]{2,1,0:T(4,128)(2,1)S(1)} %bitcast.46), channel_id=3, replica_groups=mesh['ctx'=16,'row'=4,'col'=4] {'row'}, dimensions={0}, use_global_device_ids=true | all-gather | bytes 6120 | tf_op jit(solution)/shard_map/all_gather | solution.py:21
  85.1 22.4 %all_gather.22 = bf16[16,4,153]{2,1,0:T(4,128)(2,1)S(1)} all-gather(bf16[1,4,153]{2,1,0:T(4,128)(2,1)S(1)} %psum.7), channel_id=1, replica_groups=mesh['ctx'=16,'row'=4,'col'=4] {'ctx'}, dimensions={0}, use_global_device_ids=true | all-gather | bytes 20808 | tf_op jit(solution)/shard_map/all_gather | solution.py:92
  107.5 0.1 select_reduce_fusion
  107.6 2.1 convert_reduce_fusion
  109.7 0.1 broadcast_in_dim.68
  109.8 0.2 while.12
  110.0 0.5 fusion.15
  110.6 26.1 %all-gather.12.cloned.1.call-done = bf16[16,153,2048]{2,1,0:T(8,128)(2,1)} async-done(((bf16[1,153,2048]{2,1,0:T(8,128)(2,1)}), bf16[16,153,2048]{2,1,0:T(8,128)(2,1)}) %all-gather.12.cloned.1.call-update) | async-done | bytes 10027024 | tf_op jit(solution)/shard_map/all_gather | solution.py:89
  136.7 6.8 %fusion = f32[153,2048]{1,0:T(8,128)S(1)} fusion(bf16[16,153,2048]{2,1,0:T(8,128)(2,1)} %all-gather.12.cloned.1.call-done, pred[16]{0:T(512)(128)(4,1)S(1)} %iota_compare_fusion.1), kind=kLoop, calls=%fused_computation.7 | loop fusion | flops 14727168 | bytes 11280400 | tf_op jit(solution)/shard_map/reduce_sum | solution.py:97
  143.5 0.2 add.68
  143.7 0.8 reshape.56
  144.6 3.7 %fusion.6 = f32[4,512,256]{2,1,0:T(8,128)S(1)} fusion(f32[153,4,512]{2,1,0:T(4,128)S(1)} %reshape.56, f32[256,4,136]{0,2,1:T(8,128)S(1)} %get-tuple-element.60, f32[256,4,16]{0,2,1:T(8,128)S(1)} %get-tuple-element.56, f32[153]{0:T(256)S(1)} %pad.3.clone), kind=kOutput, calls=%fused_computation.18 | convolution fusion | flops 962906112 | bytes 3973732 | tf_op jit(solution)/shard_map/thf,fhd->thd/dot_general | solution.py:103
  148.3 1.4 fusion.5
  149.7 0.0 all-gather.10.cloned.1.call-update
  149.8 0.3 reduce-scatter.2.cloned.1.call-start
  150.0 51.7 %all-gather.10.cloned.1.call-done = bf16[1024,2048]{0,1:T(8,128)(2,1)} async-done(((bf16[256,2048]{0,1:T(8,128)(2,1)}), bf16[1024,2048]{0,1:T(8,128)(2,1)}) %all-gather.10.cloned.1.call-update) | async-done | bytes 4194320 | tf_op jit(solution)/shard_map/all_gather | solution.py:116
  201.7 14.0 %convolution_convert_fusion = bf16[1024,2048]{1,0:T(8,128)(2,1)} fusion(bf16[1024,2048]{0,1:T(8,128)(2,1)} %all-gather.10.cloned.1.call-done, bf16[2048,2048]{1,0:T(8,128)(2,1)} %param.17), kind=kOutput, calls=%fused_computation.8 | convolution fusion | flops 8592031744 | bytes 16777216 | tf_op jit(solution)/shard_map/dot_general | solution.py:115
  215.7 0.0 reduce-scatter.2.cloned.1.call-update
  215.8 51.4 %reduce-scatter.2.cloned.1.call-done = bf16[256,2048]{1,0:T(8,128)(2,1)} async-done(((bf16[1024,2048]{1,0:T(8,128)(2,1)}), bf16[256,2048]{1,0:T(8,128)(2,1)}) %reduce-scatter.2.cloned.1.call-update) | async-done | bytes 1048592 | tf_op jit(solution)/shard_map/reduce_scatter | solution.py:120
  (21 shorter events, 0.2 us)
Async XLA Ops:
  6.5 60.2 %all-gather.8.cloned.1.call-start = ((), (), s32[]{:S(2)}) async-start(), calls=%async_computation.1 | async-start | bytes 3276800 | tf_op jit(solution)/shard_map/all_gather | solution.py:83
  7.3 7.1 %collective-permute-start = (bf16[2,2176]{1,0:T(2,128)(2,1)S(1)}, bf16[2,2176]{1,0:T(2,128)(2,1)S(1)}, u32[]{:S(2)}, u32[]{:S(2)}) collective-permute-start(bf16[2,2176]{1,0:T(2,128)(2,1)S(1)} %slice.31), channel_id=1, source_target_pairs={{0,4},{4,8},{8,12},{12,16},{16,20},{20,24},{24,28},{28,32},{32,36}... | collective-permute-start | bytes 26120 | tf_op jit(solution)/shard_map/ppermute | solution.py:15
  17.4 1.0 copy-start
  20.2 1.9 copy-start.5
  21.2 1.3 copy-start.3
  22.1 1.2 copy-start.1
  26.3 43.8 %copy-start.4 = (f32[256,4,16]{0,2,1:T(8,128)S(1)}, f32[256,4,16]{0,2,1:T(8,128)}, u32[]{:S(2)}) copy-start(f32[256,4,16]{0,2,1:T(8,128)} %get-tuple-element.57) | copy-start | bytes 196612
  26.3 110.4 %all-gather.12.cloned.1.call-start = ((), (), s32[]{:S(2)}) async-start(), calls=%async_computation.4 | async-start | bytes 11141120 | tf_op jit(solution)/shard_map/all_gather | solution.py:89
  70.0 131.7 %all-gather.10.cloned.1.call-start = ((), (), s32[]{:S(2)}) async-start(), calls=%async_computation.2 | async-start | bytes 5242880 | tf_op jit(solution)/shard_map/all_gather | solution.py:116
  144.6 3.7 %copy-start.2 = (bf16[256,2176]{0,1:T(8,128)(2,1)S(1)}, bf16[256,2176]{0,1:T(8,128)(2,1)}, u32[]{:S(2)}) copy-start(bf16[256,2176]{0,1:T(8,128)(2,1)} %copy-done) | copy-start | bytes 3342340
  144.6 3.7 %copy-start.6 = (bf16[4,256,256]{1,2,0:T(8,128)(2,1)S(1)}, bf16[4,256,256]{1,2,0:T(8,128)(2,1)}, u32[]{:S(2)}) copy-start(bf16[4,256,256]{1,2,0:T(8,128)(2,1)} %get-tuple-element.63) | copy-start | bytes 1572868
  149.8 117.4 %reduce-scatter.2.cloned.1.call-start = ((), (), s32[]{:S(2)}) async-start(), calls=%async_computation.3 | async-start | bytes 5242880 | tf_op jit(solution)/shard_map/reduce_scatter | solution.py:120
Sparse Core Ops, SparseCore 0:
  26.5 40.2 all-gather.7
  70.1 66.5 all-gather.11
  149.9 51.7 all-gather.9
  215.9 51.2 reduce-scatter.1
